TPU v7x, 128 devices: a whole 4x4x4 slice. The times are simulated.
128 devices in a mesh: dom: 32 (over y, x, core), rep: 4 (over z).
Axes of the slice: x: 4, y: 4, z: 4, core: 2. Of those that a mesh axis runs over, the one named last changes fastest.
Arguments:
- features: bfloat16 [4, 65536, 512], P('rep', 'dom'), may hold values from -6 to 6
- w_self: bfloat16 [512, 512], replicated, may hold values from -0.25 to 0.25
- w_neigh: bfloat16 [512, 512], replicated, may hold values from -1 to 1
- out_bias: float32 [512], replicated, may hold values from -3 to 3
- cluster_plan: int32 [512], P('dom'), may hold values from 0 to 511, as said below
- local_source: int32 [512, 3], P('dom'), may hold values from 0 to 15
- halo_owner: int32 [512, 2], P('dom'), may hold values from 0 to 31, all different within a row; in each aligned block of 16 rows (0 to 15, 16 to 31, ...) at most 2 rows name the same one
- halo_local: int32 [512, 2], P('dom'), may hold values from 0 to 15
- adjacency: bfloat16 [512, 5, 128, 128], P('dom'), may hold values from 0 to 1, as said below
- cotangent: bfloat16 [4, 65536, 512], P('rep', 'dom'), may hold values from -6 to 6
Outputs:
- new_features: bfloat16 [4, 65536, 512], P('rep', 'dom')
- feature_grad: bfloat16 [4, 65536, 512], P('rep', 'dom')
- w_self_grad: float32 [512, 512], replicated
- w_neigh_grad: float32 [512, 512], replicated
- bias_grad: float32 [512], replicated
Inputs may be any that keep to these rules, and one draw needn't show every extreme that they name: `cluster_plan`: cluster c has home partition c // 16. Every cluster stands in exactly one slot. The first 13 slots of every partition hold its own clusters in home order; its slot 13 + j holds the cluster of the same home index on the partition o_j positions further along dom (cyclically), with o_j nonzero and different for different j and the same for all partitions. `halo_owner`: each row names 2 different partitions; the 16 rows of one partition name one partition at most 2 times. `adjacency`: entries are 0 or 1.
All inputs are finite; a program needn't handle non-finite values.
Results may differ from a plain program's by a relative error of at most 0.0059.
Values may be sent and summed in bfloat16 or wider, within the bound.
A program may use at most 192 MiB of HBM per device.

v0:
```python
import math

import jax
import jax.numpy as jnp
from jax import lax
from jax.sharding import PartitionSpec as P


def pick_rows(wanted, home_index, capacity):
    wanted_int = wanted.astype(jnp.int32)
    order_of = jnp.cumsum(wanted_int, axis=1) - 1
    hits = wanted_int[:, :, None] * (
        order_of[:, :, None] == jnp.arange(capacity, dtype=jnp.int32)[None, None, :]
    ).astype(jnp.int32)
    chosen = jnp.sum(hits * home_index[:, :, None], axis=1)
    present = jnp.sum(hits, axis=1) > 0
    return (chosen, present)


def body(
    features,
    w_self,
    w_neigh,
    out_bias,
    cluster_plan,
    local_source,
    halo_owner,
    halo_local,
    adjacency,
    cotangent,
):
    dom_count = lax.axis_size("dom")
    rep_count = lax.axis_size("rep")
    my_index = lax.axis_index("dom")
    clusters = cluster_plan.shape[0]
    tile_rows = adjacency.shape[2]
    feat_width = features.shape[2]
    n_local = local_source.shape[1]
    n_halo = halo_owner.shape[1]
    capacity = max(2, 3 * clusters * n_halo // (2 * dom_count))
    home = features[0].reshape(clusters, tile_rows, feat_width)
    peers = jnp.arange(dom_count, dtype=jnp.int32)
    all_owner, all_local, all_plan = (
        lax.all_gather(halo_owner, "dom", axis=0, tiled=True),
        lax.all_gather(halo_local, "dom", axis=0, tiled=True),
        lax.all_gather(cluster_plan, "dom", axis=0, tiled=True),
    )
    halo_chosen, halo_present = pick_rows(
        all_owner.reshape(dom_count, -1) == my_index, all_local.reshape(dom_count, -1), capacity
    )
    plan_table = all_plan.reshape(dom_count, clusters)
    moved_wanted = jnp.logical_and(plan_table // clusters == my_index, peers[:, None] != my_index)
    moved_chosen, moved_present = pick_rows(moved_wanted, plan_table % clusters, 1)
    own_owner = halo_owner.reshape(-1)
    owner_onehot = (own_owner[:, None] == peers[None, :]).astype(jnp.int32)
    own_order = jnp.sum(owner_onehot * (jnp.cumsum(owner_onehot, axis=0) - 1), axis=1)
    self_owner = cluster_plan // clusters
    self_remote = self_owner != my_index

    def filled(chosen, present):
        return jnp.where(present[:, :, None, None], home[chosen], jnp.zeros((), jnp.bfloat16))

    got_halo = lax.all_to_all(
        filled(halo_chosen, halo_present), "dom", split_axis=0, concat_axis=0, tiled=True
    )
    halo_rows = got_halo[own_owner, own_order]
    got_moved = lax.all_to_all(
        filled(moved_chosen, moved_present), "dom", split_axis=0, concat_axis=0, tiled=True
    )
    moved_rows = got_moved[self_owner, 0]
    own_rows = jnp.where(self_remote[:, None, None], moved_rows, home[cluster_plan % clusters])
    neighbour = jnp.concatenate(
        [home[local_source], halo_rows.reshape(clusters, n_halo, tile_rows, feat_width)], axis=1
    )
    aggregate = jnp.einsum(
        "ckij,ckjd->cid", adjacency, neighbour, preferred_element_type=jnp.float32
    )
    degree = jnp.sum(adjacency.astype(jnp.float32), axis=(1, 3))
    scale = 1.0 / (1.0 + degree)
    neigh_mean = ((own_rows.astype(jnp.float32) + aggregate) * scale[:, :, None]).astype(
        jnp.bfloat16
    )
    own_flat = own_rows.reshape(clusters * tile_rows, feat_width)
    mean_flat = neigh_mean.reshape(clusters * tile_rows, feat_width)
    pre_act = (
        jnp.dot(own_flat, w_self, preferred_element_type=jnp.float32)
        + jnp.dot(mean_flat, w_neigh, preferred_element_type=jnp.float32)
        + out_bias
    )
    output_rows = jax.nn.silu(pre_act).astype(jnp.bfloat16)
    sig_pre = jax.nn.sigmoid(pre_act)
    grad_pre = (
        cotangent[0].astype(jnp.float32) * sig_pre * (1.0 + pre_act * (1.0 - sig_pre))
    ).astype(jnp.bfloat16)
    grad_pre = lax.optimization_barrier(grad_pre)
    grad_mean = (
        jnp.dot(grad_pre, w_neigh.T, preferred_element_type=jnp.float32)
        * scale.reshape(-1)[:, None]
    ).astype(jnp.bfloat16)
    grad_mean = lax.optimization_barrier(grad_mean)
    grad_own = (
        jnp.dot(grad_pre, w_self.T, preferred_element_type=jnp.float32)
        + grad_mean.astype(jnp.float32)
    ).astype(jnp.bfloat16)
    grad_own = grad_own.reshape(clusters, tile_rows, feat_width)
    grad_neighbour = jnp.einsum(
        "ckij,cid->ckjd",
        adjacency,
        grad_mean.reshape(clusters, tile_rows, feat_width),
        preferred_element_type=jnp.float32,
    ).astype(jnp.bfloat16)
    grad_home = jnp.zeros((clusters, tile_rows, feat_width), jnp.float32)
    grad_home = grad_home.at[local_source].add(grad_neighbour[:, :n_local].astype(jnp.float32))
    kept_own = jnp.where(self_remote[:, None, None], 0.0, grad_own.astype(jnp.float32))
    grad_home = grad_home.at[cluster_plan % clusters].add(kept_own)
    stride = capacity + 1
    send_back = jnp.zeros((dom_count * stride, tile_rows, feat_width), jnp.bfloat16)
    send_back = send_back.at[own_owner * stride + own_order].set(
        grad_neighbour[:, n_local:].reshape(-1, tile_rows, feat_width)
    )
    moved_target = jnp.where(self_remote, self_owner * stride + capacity, dom_count * stride)
    send_back = send_back.at[moved_target].set(grad_own, mode="drop")
    returned = lax.all_to_all(
        send_back.reshape(dom_count, stride, tile_rows, feat_width),
        "dom",
        split_axis=0,
        concat_axis=0,
        tiled=True,
    )
    chosen_all = jnp.concatenate([halo_chosen, moved_chosen], axis=1).reshape(-1)
    present_all = jnp.concatenate([halo_present, moved_present], axis=1).reshape(-1)
    incoming = jnp.where(
        present_all[:, None, None],
        returned.reshape(-1, tile_rows, feat_width).astype(jnp.float32),
        0.0,
    )
    grad_home = grad_home.at[chosen_all].add(incoming)
    feature_grad = grad_home.astype(jnp.bfloat16).reshape(1, clusters * tile_rows, feat_width)
    dws_part = jnp.dot(own_flat.T, grad_pre, preferred_element_type=jnp.float32)
    dwn_part = jnp.dot(mean_flat.T, grad_pre, preferred_element_type=jnp.float32)
    bias_part = jnp.sum(grad_pre.astype(jnp.float32), axis=0)
    dws_sum, dwn_sum, bias_sum = lax.psum((dws_part, dwn_part, bias_part), ("dom", "rep"))
    factor = 1.0 / math.sqrt(dom_count * rep_count * clusters * tile_rows)
    new_features = output_rows.reshape(1, clusters * tile_rows, feat_width)
    return (new_features, feature_grad, dws_sum * factor, dwn_sum * factor, bias_sum * factor)


def solution(mesh):
    return jax.shard_map(
        body,
        mesh=mesh,
        in_specs=(
            P("rep", "dom", None),
            P(),
            P(),
            P(),
            P("dom"),
            P("dom", None),
            P("dom", None),
            P("dom", None),
            P("dom", None, None, None),
            P("rep", "dom", None),
        ),
        out_specs=(P("rep", "dom", None), P("rep", "dom", None), P(), P(), P()),
        check_vma=False,
    )
```

profile of v0, /device:TPU:1, one launch (start us, length us, event | category | flops | bytes accessed | tf_op | source)
XLA Modules:
  0.0 673.6 jit_solution(7162513088943950379)
XLA Ops:
  10.1 14.4 %all-reduce.1 = s32[512]{0:T(512)S(1)} all-reduce(s32[512]{0:T(512)S(1)} %dynamic-update-slice), channel_id=1, replica_groups=mesh['dom'=32,'rep'=4] {'dom'}, use_global_device_ids=true, to_apply=%add.1 | all-reduce | flops 512 | bytes 4096
  32.3 8.5 %all-to-all-start = ((bf16[32,1,128,512]{3,2,1,0:T(8,128)(2,1)}), bf16[32,1,128,512]{3,2,1,0:T(8,128)(2,1)}, u32[]{:S(2)}, u32[]{:S(2)}) async-start(bf16[32,1,128,512]{3,2,1,0:T(8,128)(2,1)} %bitcast_select_fusion), calls=%async_computation | async-start | bytes 8388608 | tf_op jit(solution)/shard_map/all_to_all | solution.py:67
  40.9 66.7 %all-gather.1 = s32[32,16,2]{1,2,0:T(2,128)S(1)} all-gather(s32[1,16,2]{1,2,0:T(2,128)S(1)} %bitcast.108), channel_id=1, replica_groups=mesh['dom'=32,'rep'=4] {'dom'}, dimensions={0}, use_global_device_ids=true | all-gather | bytes 4224 | tf_op jit(solution)/shard_map/all_gather | solution.py:45
  107.7 23.4 %all-gather = s32[32,16,2]{1,2,0:T(2,128)S(1)} all-gather(s32[1,16,2]{1,2,0:T(2,128)S(1)} %bitcast.106), channel_id=1, replica_groups=mesh['dom'=32,'rep'=4] {'dom'}, dimensions={0}, use_global_device_ids=true | all-gather | bytes 4224 | tf_op jit(solution)/shard_map/all_gather | solution.py:44
  132.0 5.4 gather_fusion.4
  137.4 7.2 %broadcast_select_fusion = bf16[32,2,128,512]{3,2,1,0:T(8,128)(2,1)} fusion(bf16[32,2,128,512]{3,2,1,0:T(8,128)(2,1)} %bitcast.96, pred[32,2]{1,0:T(8,128)(4,1)S(1)} %copy.74), kind=kLoop, calls=%fused_computation.17 | loop fusion | flops 4194304 | bytes 16777280 | tf_op jit(solution)/shard_map/jit(_where)/select_n | solution.py:61
  144.6 5.1 all-to-all-start.1
  169.7 79.4 %all-to-all-done.1 = bf16[32,2,128,512]{3,2,1,0:T(8,128)(2,1)} async-done(((bf16[32,2,128,512]{3,2,1,0:T(8,128)(2,1)}), bf16[32,2,128,512]{3,2,1,0:T(8,128)(2,1)}, u32[]{:S(2)}, u32[]{:S(2)}) %all-to-all-start.1) | async-done | bytes 8388640 | tf_op jit(solution)/shard_map/all_to_all | solution.py:63
  249.1 6.1 gather_fusion.5
  255.2 7.4 %fusion.7 = bf16[16,128,512]{2,1,0:T(8,128)(2,1)S(1)} fusion(bf16[16,5,128,128]{3,2,1,0:T(8,128)(2,1)} %param.18, bf16[16,2,128,512]{3,2,1,0:T(8,128)(2,1)} %bitcast.101, bf16[16,3,128,512]{3,2,1,0:T(8,128)(2,1)} %bitcast.100, f32[16,128]{1,0:T(8,128)S(1)} %get-tuple-element.16, bf16[16,128,512]{2,1,0:T(8,128)(2,1)} %gather_fusion.1, ...), kind=kOutput, calls=%fused_computation.25 | convolution fusion | flops 1368391680 | bytes 19406864 | tf_op jit(solution)/shard_map/ckij,ckjd->cid/dot_general | solution.py:75
  270.6 5.3 convert_bitcast_fusion
  282.3 6.4 copy.84
  288.8 6.0 broadcast_in_dim.118
  294.8 11.4 %scatter_fusion.2 = bf16[96,128,512]{2,1,0:T(8,128)(2,1)} fusion(bf16[96,128,512]{2,1,0:T(8,128)(2,1)} %broadcast_in_dim.118, s32[32]{0:T(128)S(1)} %get-tuple-element.17, bf16[32,128,512]{2,1,0:T(8,128)(2,1)} %copy.84), kind=kCustom, calls=%fused_computation.8 | custom fusion | bytes 12583040 | tf_op jit(solution)/shard_map/scatter | solution.py:118
  306.2 5.0 scatter_fusion.3
  311.2 11.3 %all-to-all-start.2 = ((bf16[32,3,128,512]{3,2,1,0:T(8,128)(2,1)}), bf16[32,3,128,512]{3,2,1,0:T(8,128)(2,1)}, u32[]{:S(2)}, u32[]{:S(2)}) async-start(bf16[32,3,128,512]{3,2,1,0:T(8,128)(2,1)} %bitcast.94), calls=%async_computation.2 | async-start | bytes 25165824 | tf_op jit(solution)/shard_map/all_to_all | solution.py:123
  329.9 8.8 %slice_convert_fusion = f32[16,3,128,512]{2,3,1,0:T(8,128)} fusion(bf16[16,5,128,512]{2,3,1,0:T(8,128)(2,1)} %copy-done.2), kind=kLoop, calls=%fused_computation.18 | loop fusion | flops 3145728 | bytes 18874368 | tf_op jit(solution)/shard_map/convert_element_type | solution.py:113
  338.8 12.6 %copy.81 = f32[16,3,128,512]{3,2,1,0:T(8,128)} copy(f32[16,3,128,512]{2,3,1,0:T(8,128)} %slice_convert_fusion) | data formatting | bytes 25165824 | tf_op jit(solution)/shard_map/convert_element_type | solution.py:113
  353.9 27.6 %scatter_fusion = f32[16,128,512]{2,1,0:T(8,128)} fusion(f32[16,128,512]{2,1,0:T(8,128)} %broadcast_in_dim.115, s32[48]{0:T(128)S(1)} %reshape.323, f32[48,128,512]{2,1,0:T(8,128)} %bitcast.95), kind=kCustom, calls=%fused_computation.6 | custom fusion | flops 3145728 | bytes 37748928 | tf_op jit(solution)/shard_map/scatter-add | solution.py:113
  384.1 9.8 %scatter_fusion.1 = f32[16,128,512]{2,1,0:T(8,128)} fusion(f32[16,128,512]{2,1,0:T(8,128)} %scatter_fusion, s32[16]{0:T(128)S(1)} %get-tuple-element.21, f32[16,128,512]{2,1,0:T(8,128)} %convert_select_fusion.1), kind=kCustom, calls=%fused_computation.7 | custom fusion | flops 1048576 | bytes 12582976 | tf_op jit(solution)/shard_map/scatter-add | solution.py:115
  394.3 143.6 %psum.23 = f32[512]{0:T(512)S(1)} all-reduce(f32[512]{0:T(512)S(1)} %convert_reduce_fusion.1), channel_id=1, replica_groups=mesh['dom'=32,'rep'=4] {'dom','rep'}, use_global_device_ids=true, to_apply=%region_17.18 | all-reduce | flops 512 | bytes 4096 | tf_op jit(solution)/shard_map/psum | solution.py:142
  538.5 55.8 %all-reduce.5.cloned.1.call-done = (f32[512,512]{1,0:T(8,128)}, f32[512,512]{1,0:T(8,128)}) async-done(((f32[512,512]{1,0:T(8,128)}, f32[512,512]{1,0:T(8,128)}), (f32[512,512]{1,0:T(8,128)}, f32[512,512]{1,0:T(8,128)})) %all-reduce.5.cloned.1.call-update) | async-done | bytes 2097168 | tf_op jit(solution)/shard_map/psum | solution.py:142
  597.3 14.5 %convert_select_fusion = f32[96,128,512]{2,1,0:T(8,128)} fusion(bf16[32,3,128,512]{3,2,1,0:T(8,128)(2,1)} %all-to-all-done.2, pred[96]{0:T(512)(128)(4,1)S(1)} %broadcast_in_dim.116), kind=kLoop, calls=%fused_computation.11 | loop fusion | flops 12582912 | bytes 37748832 | tf_op jit(solution)/shard_map/jit(_where)/select_n | solution.py:132
  611.9 51.1 %scatter_fusion.4 = f32[16,128,512]{2,1,0:T(8,128)} fusion(f32[16,128,512]{2,1,0:T(8,128)} %scatter_fusion.1, s32[96]{0:T(128)S(1)} %fusion.28, f32[96,128,512]{2,1,0:T(8,128)} %convert_select_fusion), kind=kCustom, calls=%fused_computation.10 | custom fusion | flops 6291456 | bytes 75497856 | tf_op jit(solution)/shard_map/scatter-add | solution.py:137
  (110 shorter events, 65.7 us)
Async XLA Ops:
  7.2 18.0 %copy-start = (bf16[1,2048,512]{2,1,0:T(8,128)(2,1)S(1)}, bf16[1,2048,512]{2,1,0:T(8,128)(2,1)}, u32[]{:S(2)}) copy-start(bf16[1,2048,512]{2,1,0:T(8,128)(2,1)} %param.10) | copy-start | bytes 6291460
  32.3 8.5 %copy-start.12 = (s32[16,2]{0,1:T(2,128)S(1)}, s32[16,2]{0,1:T(2,128)}, u32[]{:S(2)}) copy-start(s32[16,2]{0,1:T(2,128)} %param.17) | copy-start | bytes 388
  32.3 75.4 %copy-start.10 = (s32[16,2]{0,1:T(2,128)S(1)}, s32[16,2]{0,1:T(2,128)}, u32[]{:S(2)}) copy-start(s32[16,2]{0,1:T(2,128)} %param.16) | copy-start | bytes 388
  32.3 112.3 %all-to-all-start = ((bf16[32,1,128,512]{3,2,1,0:T(8,128)(2,1)}), bf16[32,1,128,512]{3,2,1,0:T(8,128)(2,1)}, u32[]{:S(2)}, u32[]{:S(2)}) async-start(bf16[32,1,128,512]{3,2,1,0:T(8,128)(2,1)} %bitcast_select_fusion), calls=%async_computation | async-start | bytes 8388608 | tf_op jit(solution)/shard_map/all_to_all | solution.py:67
  144.6 5.4 copy-start.11
  144.6 5.7 copy-start.13
  144.6 104.5 %all-to-all-start.1 = ((bf16[32,2,128,512]{3,2,1,0:T(8,128)(2,1)}), bf16[32,2,128,512]{3,2,1,0:T(8,128)(2,1)}, u32[]{:S(2)}, u32[]{:S(2)}) async-start(bf16[32,2,128,512]{3,2,1,0:T(8,128)(2,1)} %broadcast_select_fusion), calls=%async_computation.1 | async-start | bytes 16777216 | tf_op jit(solution)/shard_map/all_to_all | solution.py:63
  163.9 2.5 copy-start.9
  255.2 7.4 %copy-start.4 = (f32[2048,512]{1,0:T(8,128)S(1)}, f32[2048,512]{1,0:T(8,128)}, u32[]{:S(2)}) copy-start(f32[2048,512]{1,0:T(8,128)} %fusion.34) | copy-start | bytes 12582916
  255.2 7.9 %copy-start.14 = (bf16[1,2048,512]{2,1,0:T(8,128)(2,1)S(1)}, bf16[1,2048,512]{2,1,0:T(8,128)(2,1)}, u32[]{:S(2)}) copy-start(bf16[1,2048,512]{2,1,0:T(8,128)(2,1)} %param.19) | copy-start | bytes 6291460
  255.2 8.0 %copy-start.15 = (bf16[512,512]{1,0:T(8,128)(2,1)S(1)}, bf16[512,512]{1,0:T(8,128)(2,1)}, u32[]{:S(2)}) copy-start(bf16[512,512]{1,0:T(8,128)(2,1)} %param.12) | copy-start | bytes 1572868
  255.2 8.0 %copy-start.16 = (f32[512]{0:T(512)S(1)}, f32[512]{0:T(512)}, u32[]{:S(2)}) copy-start(f32[512]{0:T(512)} %param.13) | copy-start | bytes 6148
  262.6 4.1 copy-start.17
  266.7 1.3 copy-start.5
  268.0 2.6 copy-start.8
  275.9 4.0 copy-start.2
  311.2 286.2 %all-to-all-start.2 = ((bf16[32,3,128,512]{3,2,1,0:T(8,128)(2,1)}), bf16[32,3,128,512]{3,2,1,0:T(8,128)(2,1)}, u32[]{:S(2)}, u32[]{:S(2)}) async-start(bf16[32,3,128,512]{3,2,1,0:T(8,128)(2,1)} %bitcast.94), calls=%async_computation.2 | async-start | bytes 25165824 | tf_op jit(solution)/shard_map/all_to_all | solution.py:123
  322.5 271.7 %all-reduce.5.cloned.1.call-start = ((), (), s32[]{:S(2)}) async-start(), calls=%async_computation.3 | async-start | bytes 4194304 | tf_op jit(solution)/shard_map/psum | solution.py:142
  323.0 4.6 copy-start.6
  353.9 27.6 %copy-start.3 = (bf16[2048,512]{1,0:T(8,128)(2,1)S(1)}, bf16[2048,512]{1,0:T(8,128)(2,1)}, u32[]{:S(2)}) copy-start(bf16[2048,512]{1,0:T(8,128)(2,1)} %add_convert_fusion) | copy-start | bytes 6291460
  384.1 9.8 %copy-start.7 = (bf16[2048,512]{1,0:T(8,128)(2,1)S(1)}, bf16[2048,512]{1,0:T(8,128)(2,1)}, u32[]{:S(2)}) copy-start(bf16[2048,512]{1,0:T(8,128)(2,1)} %copy-done.5) | copy-start | bytes 6291460
  611.9 54.9 %copy-start.1 = (bf16[1,2048,512]{2,1,0:T(8,128)(2,1)S(1)}, bf16[1,2048,512]{2,1,0:T(8,128)(2,1)}, u32[]{:S(2)}) copy-start(bf16[1,2048,512]{2,1,0:T(8,128)(2,1)} %param.10) | copy-start | bytes 6291460
Sparse Core Ops, SparseCore 0:
  330.1 264.1 all-reduce.4
where the time goes:
time: 676 us; the launch traced here: 674 us
  blocking collectives  248 us (37%)
  other arithmetic  140 us (21%)
  waiting for transfers between devices  135 us (20%)
  local copies, waits for them, and re-layouts  80.2 us (12%)
  matrix products  30.2 us (4%)
  starting transfers between devices  25 us (4%)
  between operations  15 us (2%)
    psum x1, blocking collectives, body(): lax.psum((dws_part, dwn_part, bias_part), ('dom', 'rep'))  144 us
    all_to_all x1, waiting for transfers between devices, body(): lax.all_to_all(filled(halo_chosen, halo_present), 'dom', split_axis=0, co...  79.4 us
    all_gather x1, blocking collectives, body(): lax.all_gather(halo_local, 'dom', axis=0, tiled=True)  66.7 us
    psum x1, waiting for transfers between devices, body(): lax.psum((dws_part, dwn_part, bias_part), ('dom', 'rep'))  55.8 us
    scatter-add x1, other arithmetic, body(): grad_home = grad_home.at[chosen_all].add(incoming)  51.1 us
    scatter-add x1, other arithmetic, body(): grad_home.at[local_source]  27.6 us
    all_gather x1, blocking collectives, body(): lax.all_gather(halo_owner, 'dom', axis=0, tiled=True)  23.4 us
    select_n x1, other arithmetic, body(): jnp.where(present_all[:, None, None], returned.reshape(-1, tile_rows, fea...  14.5 us
  transfers between devices with their start and end apart: 4, of which 2 were waited for; matrix products, arithmetic and copies ran while one was open for 16% of the time, Pallas kernels for 0%

commit v1 on v0

v1 whole, which is shorter than its diff:
```python
import functools
import math

import jax
import jax.numpy as jnp
from jax import lax
from jax.experimental import pallas as pl
from jax.experimental.pallas import tpu as pltpu
from jax.sharding import PartitionSpec as P

D = 512
TILE = 128
CL = 16
KL = 3
KH = 2
MIG = 3
OWN = CL - MIG
NDOM = 32
NREP = 4
HALF = TILE // 2
WIDE = TILE + HALF
CHUNK = 16
SIDE = 4
GROUP = 4
STEPS = CL // GROUP
ROWS = GROUP * TILE
MESH = pl.DeviceIdType.MESH
F32 = jnp.float32
BF16 = jnp.bfloat16

ANY = pl.BlockSpec(memory_space=pl.ANY)
VMEM = pl.BlockSpec(memory_space=pltpu.VMEM)
SMEM = pl.BlockSpec(memory_space=pltpu.SMEM)


def dot_tn(a, b):
    return lax.dot_general(a, b, (((0,), (0,)), ((), ())), preferred_element_type=F32)


def dot_nt(a, b):
    return lax.dot_general(a, b, (((1,), (1,)), ((), ())), preferred_element_type=F32)


def dot_nn(a, b):
    return jnp.dot(a, b, preferred_element_type=F32)


ZROWS = D // NREP
CHIPS = NDOM // 2
CROWS = ZROWS // CHIPS

ORDER = [
    (1, 0), (3, 0), (0, 1), (0, 3), (1, 1), (3, 3), (1, 3), (3, 1),
    (2, 0), (0, 2), (2, 2), (1, 2), (2, 1), (3, 2), (2, 3),
]
PEERS = [(0, 0, 1)] + [(dx, dy, dc) for dx, dy in ORDER for dc in (0, 1)]
NPEER = len(PEERS)


class Place:
    def __init__(self):
        self.me, self.rep = lax.axis_index("dom"), lax.axis_index("rep")
        self.core, self.chip = lax.rem(self.me, 2), self.me // 2
        self.x, self.y = lax.rem(self.chip, SIDE), self.chip // SIDE
        self.partner = self.chip * 2 + 1 - self.core

    def at(self, dx, dy, dc):
        x, y = lax.rem(self.x + dx, SIDE), lax.rem(self.y + dy, SIDE)
        return (y * SIDE + x) * 2 + lax.rem(self.core + dc, 2)


def loop(low, high, f):
    def step(t, carry):
        f(t)
        return carry

    lax.fori_loop(low, high, step, 0)


def greet_plane(here, barrier):
    def one(t):
        dom = lax.rem(here.me + t, NDOM)
        pl.semaphore_signal(barrier, inc=1, device_id=(dom, here.rep), device_id_type=MESH)

    loop(1, NDOM, one)


def remote(src, dst, send_sem, recv_sem, dom, z):
    return pltpu.make_async_remote_copy(
        src_ref=src,
        dst_ref=dst,
        send_sem=send_sem,
        recv_sem=recv_sem,
        device_id=(dom, z),
        device_id_type=MESH,
    )


class Exchange:
    def __init__(self, here, src, dst, send_sem, recv_sem, first, last):
        self.here, self.src, self.dst = here, src, dst
        self.send_sem, self.recv_sem = send_sem, recv_sem
        self.first, self.last = first, last

    def copy(self, n, rows):
        dom = self.here.at(*PEERS[n])
        return remote(
            self.src.at[dom, rows],
            self.dst.at[self.here.me, rows],
            self.send_sem.at[n],
            self.recv_sem.at[n],
            dom,
            self.here.rep,
        )

    def start(self, low, high):
        def chunk(c):
            rows = pl.ds(pl.multiple_of(self.first + c * CHUNK, CHUNK), CHUNK)
            for n in range(NPEER):
                self.copy(n, rows).start()

        loop(low, high, chunk)

    def every(self, n):
        return self.copy(n, pl.ds(self.first, self.last - self.first))


class Shift:
    def __init__(self, here, pick_ref, along_x, picked, along_y, lanes, sems):
        self.here, self.pick = here, pick_ref
        self.along_x, self.picked, self.along_y, self.lanes = along_x, picked, along_y, lanes
        self.sems = sems

    def sem(self, n):
        return self.sems.at[0, n], self.sems.at[1, n]

    def copy_x(self, t):
        here = self.here
        slot = self.along_x.at[here.x]
        return remote(slot, slot, *self.sem(t), here.at(t, 0, 0), here.rep)

    def copy_y(self, t):
        here = self.here
        return remote(
            self.picked, self.along_y.at[here.y], *self.sem(SIDE + t), here.at(0, t, 0), here.rep
        )

    def copy_lane(self):
        here = self.here
        slot = self.lanes.at[here.core]
        return remote(slot, slot, *self.sem(0), here.partner, here.rep)

    def start_x(self):
        loop(1, SIDE, lambda t: self.copy_x(t).start())

    def start_y(self):
        loop(1, SIDE, lambda t: self.copy_x(t).wait())
        for j in range(MIG):
            self.picked[j] = self.along_x[self.pick[j], j]
        self.along_y[self.here.y] = self.picked[...]
        loop(1, SIDE, lambda t: self.copy_y(t).start())

    def start_lane(self):
        loop(1, SIDE, lambda t: self.copy_y(t).wait())
        for j in range(MIG):
            self.lanes[self.here.core, j] = self.along_y[self.pick[MIG + j], j]
        self.copy_lane().start()

    def finish(self, out_ref):
        self.copy_lane().wait()
        for j in range(MIG):
            out_ref[j] = self.lanes[lax.rem(self.here.core + self.pick[2 * MIG + j], 2), j]


SHIFT_SCRATCH = [
    pltpu.VMEM((SIDE, MIG, TILE, D), BF16),
    pltpu.VMEM((MIG, TILE, D), BF16),
    pltpu.VMEM((SIDE, MIG, TILE, D), BF16),
    pltpu.VMEM((2, MIG, TILE, D), BF16),
    pltpu.SemaphoreType.DMA((2, 2 * SIDE)),
]
EXCHANGE_SEMS = pltpu.SemaphoreType.DMA((2, NPEER))


def forward_kernel(
    pick_ref, row_ref, home_ref,
    recv_ref, table_ref, moved_ref,
    feat, stage, asked, along_x, picked, along_y, lanes, shift_sems,
    table_sems, tile_sems, local_sems,
):
    here = Place()
    me, core, rep = here.me, here.core, here.rep
    barrier = pltpu.get_barrier_semaphore()
    greet_plane(here, barrier)
    own = feat.at[pl.ds(core * CL, CL)]
    take = pltpu.make_async_copy(home_ref, own, local_sems.at[0])
    take.start()
    mine = pltpu.make_async_copy(home_ref.at[pl.ds(OWN, MIG)], along_x.at[here.x], local_sems.at[1])
    mine.start()
    table_ref[me] = row_ref[...]
    pl.semaphore_wait(barrier, NDOM - 1)

    def table(n):
        return remote(
            row_ref, table_ref.at[me], table_sems.at[0, n], table_sems.at[1, n],
            lax.rem(me + n, NDOM), rep,
        )

    loop(1, NDOM, lambda n: table(n).start())
    share = remote(home_ref, own, local_sems.at[2], local_sems.at[3], here.partner, rep)
    share.start()
    shift = Shift(here, pick_ref, along_x, picked, along_y, lanes, shift_sems)
    mine.wait()
    shift.start_x()
    loop(1, NDOM, lambda n: table(n).wait())
    read = pltpu.make_async_copy(table_ref, asked, local_sems.at[4])
    read.start()
    read.wait()
    take.wait()
    share.wait()

    def gather(p):
        first = asked[p, 0, me]
        other = asked[p, 0, NDOM + here.chip]
        stage[p, pl.ds(0, TILE)] = feat[core * CL + jnp.maximum(first, 0)]
        stage[p, pl.ds(TILE, HALF)] = feat[
            jnp.maximum(other, 0), pl.ds(pl.multiple_of(core * HALF, HALF), HALF)
        ]

    loop(0, NDOM, gather)
    keep = pltpu.make_async_copy(stage.at[me], recv_ref.at[me], local_sems.at[5])
    keep.start()
    tiles = Exchange(here, stage, recv_ref, tile_sems.at[0], tile_sems.at[1], 0, WIDE)
    tiles.start(0, 4)
    shift.start_y()
    tiles.start(4, 8)
    shift.start_lane()
    tiles.start(8, WIDE // CHUNK)
    shift.finish(moved_ref)
    keep.wait()
    for n in range(NPEER):
        tiles.every(n).wait()


def exchange_forward(pick, row, home):
    return pl.pallas_call(
        forward_kernel,
        out_shape=[
            jax.ShapeDtypeStruct((NDOM, WIDE, D), BF16),
            jax.ShapeDtypeStruct((NDOM, 1, 128), jnp.int32),
            jax.ShapeDtypeStruct((MIG, TILE, D), BF16),
        ],
        in_specs=[SMEM, VMEM, ANY],
        out_specs=[ANY, VMEM, VMEM],
        scratch_shapes=[
            pltpu.VMEM((2 * CL, TILE, D), BF16),
            pltpu.VMEM((NDOM, WIDE, D), BF16),
            pltpu.SMEM((NDOM, 1, 128), jnp.int32),
        ]
        + SHIFT_SCRATCH
        + [pltpu.SemaphoreType.DMA((2, NDOM)), EXCHANGE_SEMS, pltpu.SemaphoreType.DMA((6,))],
        compiler_params=pltpu.CompilerParams(
            collective_id=0, has_side_effects=True, vmem_limit_bytes=32 * 2**20
        ),
    )(pick, row, home)


def backward_kernel(
    pick_ref, back_ref, tail_ref, dw_ref, db_ref,
    ret_ref, passed_ref, moved_ref, out_ref, bias_ref,
    along_x, picked, along_y, lanes, shift_sems,
    r1, b1, s1, r2, b2, s2, r3, b3, sums, half_sems, tile_sems, pass_sems, local_sems,
):
    here = Place()
    me, core, chip, rep, partner = here.me, here.core, here.chip, here.rep, here.partner
    barrier = pltpu.get_barrier_semaphore()

    def z_peer(t):
        return lax.rem(rep + t, NREP)

    def chip_peer(t):
        return lax.rem(chip + t, CHIPS)

    def greet_z(t):
        pl.semaphore_signal(barrier, inc=1, device_id=(me, z_peer(t)), device_id_type=MESH)

    greet_plane(here, barrier)
    loop(1, NREP, greet_z)
    keep = pltpu.make_async_copy(back_ref.at[me], ret_ref.at[me], local_sems.at[0])
    keep.start()
    along_x[here.x] = tail_ref[...]
    pl.semaphore_wait(barrier, NDOM - 1 + NREP - 1)

    def send(src, dst, n, dom, z):
        return remote(src, dst, sums.at[0, n], sums.at[1, n], dom, z)

    shift = Shift(here, pick_ref, along_x, picked, along_y, lanes, shift_sems)
    halves = Exchange(here, back_ref, ret_ref, half_sems.at[0], half_sems.at[1], TILE, WIDE)
    tiles = Exchange(here, back_ref, ret_ref, tile_sems.at[0], tile_sems.at[1], 0, TILE)

    c_dw = send(dw_ref.at[1 - core], r1, 0, partner, rep)
    c_db = send(db_ref, b1, 1, partner, rep)
    c_dw.start()
    c_db.start()
    shift.start_x()
    halves.start(0, HALF // CHUNK)
    c_db.wait()
    c_dw.wait()
    s1[...] = dw_ref[core] + r1[...]
    b2[rep] = db_ref[...] + b1[...]

    def z_dw(t):
        z = z_peer(t)
        return send(s1.at[pl.ds(z * ZROWS, ZROWS)], r2.at[rep], 2 + t, me, z)

    def z_db(t):
        return send(b2.at[rep], b2.at[rep], 6 + t, me, z_peer(t))

    loop(1, NREP, lambda t: z_dw(t).start())
    loop(1, NREP, lambda t: z_db(t).start())
    r2[rep] = s1[pl.ds(pl.multiple_of(rep * ZROWS, ZROWS), ZROWS)]
    tiles.start(0, 2)
    shift.start_y()
    loop(1, NREP, lambda t: z_db(t).wait())
    loop(1, NREP, lambda t: z_dw(t).wait())
    s2[...] = (r2[0] + r2[1]) + (r2[2] + r2[3])
    b3[chip] = (b2[0] + b2[1]) + (b2[2] + b2[3])

    def p_dw(t):
        q = chip_peer(t)
        return send(s2.at[pl.ds(q * CROWS, CROWS)], r3.at[chip], 10 + t, q * 2 + core, rep)

    def p_db(t):
        return send(b3.at[chip], b3.at[chip], 26 + t, chip_peer(t) * 2 + core, rep)

    loop(1, CHIPS, lambda t: p_dw(t).start())
    loop(1, CHIPS, lambda t: p_db(t).start())
    r3[chip] = s2[pl.ds(pl.multiple_of(chip * CROWS, CROWS), CROWS)]
    tiles.start(2, 4)
    shift.start_lane()
    loop(1, CHIPS, lambda t: p_dw(t).wait())
    total = r3[0]
    for q in range(1, CHIPS):
        total = total + r3[q]
    mine = out_ref.at[core, pl.ds(pl.multiple_of(rep * ZROWS + chip * CROWS, CROWS), CROWS)]
    mine[...] = total

    def p_out(t):
        return send(mine, mine, 42 + t, chip_peer(t) * 2 + core, rep)

    loop(1, CHIPS, lambda t: p_out(t).start())
    tiles.start(4, 6)
    shift.finish(moved_ref)
    loop(1, CHIPS, lambda t: p_db(t).wait())
    bias = b3[0]
    for q in range(1, CHIPS):
        bias = bias + b3[q]
    bias_ref[...] = bias
    loop(1, CHIPS, lambda t: p_out(t).wait())
    block = out_ref.at[core, pl.ds(pl.multiple_of(rep * ZROWS, ZROWS), ZROWS)]

    def z_out(t):
        return send(block, block, 58 + t, me, z_peer(t))

    loop(1, NREP, lambda t: z_out(t).start())
    tiles.start(6, TILE // CHUNK)

    def pass_on(src, n):
        rows = pl.ds(TILE, HALF)
        return remote(
            ret_ref.at[src, rows], passed_ref.at[src], pass_sems.at[0, n], pass_sems.at[1, n],
            partner, rep,
        )

    keep.wait()
    pass_on(me, NPEER).start()
    for n, (dx, dy, dc) in enumerate(PEERS):
        halves.every(n).wait()
        pass_on(here.at(SIDE - dx, SIDE - dy, dc), n).start()
    loop(1, NREP, lambda t: z_out(t).wait())
    last = send(out_ref.at[core], out_ref.at[core], 62, partner, rep)
    last.start()
    pass_on(me, NPEER).wait()
    for n, (dx, dy, dc) in enumerate(PEERS):
        pass_on(here.at(SIDE - dx, SIDE - dy, dc), n).wait()
    for n in range(NPEER):
        tiles.every(n).wait()
    last.wait()


def exchange_backward(pick, back, tail, dw, db):
    return pl.pallas_call(
        backward_kernel,
        out_shape=[
            jax.ShapeDtypeStruct((NDOM, WIDE, D), BF16),
            jax.ShapeDtypeStruct((NDOM, HALF, D), BF16),
            jax.ShapeDtypeStruct((MIG, TILE, D), BF16),
            jax.ShapeDtypeStruct((2, D, D), F32),
            jax.ShapeDtypeStruct((8, D), F32),
        ],
        in_specs=[SMEM, ANY, VMEM, VMEM, VMEM],
        out_specs=[ANY, ANY, VMEM, VMEM, VMEM],
        scratch_shapes=SHIFT_SCRATCH
        + [
            pltpu.VMEM((D, D), F32),
            pltpu.VMEM((8, D), F32),
            pltpu.VMEM((D, D), F32),
            pltpu.VMEM((NREP, ZROWS, D), F32),
            pltpu.VMEM((NREP, 8, D), F32),
            pltpu.VMEM((ZROWS, D), F32),
            pltpu.VMEM((CHIPS, CROWS, D), F32),
            pltpu.VMEM((CHIPS, 8, D), F32),
            pltpu.SemaphoreType.DMA((2, 64)),
            EXCHANGE_SEMS,
            EXCHANGE_SEMS,
            pltpu.SemaphoreType.DMA((2, NDOM)),
            pltpu.SemaphoreType.DMA((1,)),
        ],
        compiler_params=pltpu.CompilerParams(
            collective_id=1, has_side_effects=True, vmem_limit_bytes=32 * 2**20
        ),
    )(pick, back, tail, dw, db)


def tile_block(width=D):
    return pl.BlockSpec((GROUP, TILE, width), lambda g, *_: (g, 0, 0))


def whole(*shape):
    return pl.BlockSpec(shape, lambda g, *_: (0,) * len(shape))


def adj_block(k):
    return pl.BlockSpec((GROUP, 1, TILE, TILE), lambda g, *_: (g, k, 0, 0))


def own_tile(i, g, home_tile, moved_ref):
    j = CL - GROUP + i - OWN
    if j < 0:
        return home_tile
    return jnp.where(g == STEPS - 1, moved_ref[j], home_tile)


PARTS = 2 * GROUP * KH


def middle_kernel(block_ref, src_ref, *refs):
    halo = refs[:PARTS]
    (home_ref, moved_ref, adj_ref, cot_ref, ws_ref, wn_ref, bias_ref) = refs[PARTS : PARTS + 7]
    (new_ref, gp_ref, mean_ref, gm_ref, tail_ref, back_ref) = refs[PARTS + 7 : PARTS + 13]
    (own, scale, grads, sem) = refs[PARTS + 13 :]
    g = pl.program_id(0)
    for i in range(GROUP):
        slot = g * GROUP + i
        rows = pl.ds(i * TILE, TILE)
        mine = own_tile(i, g, home_ref[slot], moved_ref)
        own[rows] = mine
        adj = jnp.concatenate([adj_ref[i, k] for k in range(KL + KH)], axis=1)
        total = jnp.sum(adj.astype(F32), axis=1, keepdims=True)
        scale[rows] = jnp.broadcast_to(1.0 / (1.0 + total), (TILE, D))
        near = [home_ref[src_ref[slot * KL + k]] for k in range(KL)]
        far = [halo[2 * KH * i + n][0] for n in range(2 * KH)]
        agg = mine.astype(F32) + dot_nn(adj, jnp.concatenate(near + far, axis=0))
        mean_ref[i] = (agg * scale[rows]).astype(BF16)
    pre = (
        dot_nn(own[...], ws_ref[...])
        + dot_nn(mean_ref[...].reshape(ROWS, D), wn_ref[...])
        + bias_ref[...]
    )
    sig = 1.0 / (1.0 + jnp.exp(-pre))
    new_ref[...] = (pre * sig).astype(BF16).reshape(GROUP, TILE, D)
    cot = cot_ref[...].reshape(ROWS, D).astype(F32)
    gp = (cot * sig * (1.0 + pre * (1.0 - sig))).astype(BF16)
    gp_ref[...] = gp.reshape(GROUP, TILE, D)
    gm = (dot_nt(gp, wn_ref[...]) * scale[...]).astype(BF16)
    gm_ref[...] = gm.reshape(GROUP, TILE, D)

    def copy(n):
        return pltpu.make_async_copy(grads.at[n], back_ref.at[block_ref[n]], sem.at[n])

    for i in range(GROUP):
        adj = jnp.concatenate([adj_ref[i, KL + k] for k in range(KH)], axis=1)
        both = dot_tn(adj, gm[i * TILE : (i + 1) * TILE]).astype(BF16)
        for part in range(2 * KH):
            n = (g * GROUP + i) * 2 * KH + part
            grads[n] = both[part * HALF : (part + 1) * HALF]
            copy(n).start()

    @pl.when(g == STEPS - 1)
    def _():
        first = TILE * (GROUP - MIG)
        tail = dot_nt(gp[first:], ws_ref[...]) + gm[first:].astype(F32)
        tail_ref[...] = tail.astype(BF16).reshape(MIG, TILE, D)
        loop(0, 2 * CL * KH, lambda n: copy(n).wait())


def middle(blocks, src, recv, home, moved, adjacency, cot, w_self, w_neigh, bias):
    def halo_block(n):
        return pl.BlockSpec((1, HALF, D), lambda g, blocks, src: (blocks[g * PARTS + n], 0, 0))

    tiles = jax.ShapeDtypeStruct((CL, TILE, D), BF16)
    return pl.pallas_call(
        middle_kernel,
        out_shape=[
            tiles, tiles, tiles, tiles,
            jax.ShapeDtypeStruct((MIG, TILE, D), BF16),
            jax.ShapeDtypeStruct(recv.shape, BF16),
        ],
        grid_spec=pltpu.PrefetchScalarGridSpec(
            num_scalar_prefetch=2,
            grid=(STEPS,),
            in_specs=[halo_block(n) for n in range(PARTS)]
            + [
                whole(CL, TILE, D),
                whole(MIG, TILE, D),
                pl.BlockSpec((GROUP, KL + KH, TILE, TILE), lambda g, *_: (g, 0, 0, 0)),
                tile_block(),
                whole(D, D),
                whole(D, D),
                whole(1, D),
            ],
            out_specs=[tile_block()] * 4 + [whole(MIG, TILE, D), ANY],
            scratch_shapes=[
                pltpu.VMEM((ROWS, D), BF16),
                pltpu.VMEM((ROWS, D), F32),
                pltpu.VMEM((2 * CL * KH, HALF, D), BF16),
                pltpu.SemaphoreType.DMA((2 * CL * KH,)),
            ],
        ),
        compiler_params=pltpu.CompilerParams(vmem_limit_bytes=40 * 2**20),
    )(
        blocks, src, *([recv] * PARTS), home, moved, adjacency, cot, w_self, w_neigh, bias
    )


def rest_kernel(
    src_ref, gp_ref, gm_ref, home_ref, moved_ref, mean_ref, a0_ref, a1_ref, a2_ref, w_ref,
    acc_ref, dw_ref, db_ref, own,
):
    g = pl.program_id(0)

    @pl.when(g == 0)
    def _():
        acc_ref[...] = jnp.zeros_like(acc_ref)
        dw_ref[...] = jnp.zeros_like(dw_ref)
        db_ref[...] = jnp.zeros_like(db_ref)

    gp = gp_ref[...].reshape(ROWS, D)
    gm = gm_ref[...].reshape(ROWS, D)
    own_grad = (dot_nt(gp, w_ref[...]) + gm.astype(F32)).astype(BF16)
    for i in range(GROUP):
        part = own_grad[i * TILE : (i + 1) * TILE]
        slot = g * GROUP + i
        own[pl.ds(i * TILE, TILE)] = own_tile(i, g, home_ref[i], moved_ref)

        @pl.when(slot < OWN)
        def _():
            acc_ref[slot] += part.astype(F32)

        adj = jnp.concatenate([a0_ref[i, 0], a1_ref[i, 0], a2_ref[i, 0]], axis=1)
        grads = dot_tn(adj, gm[i * TILE : (i + 1) * TILE]).astype(BF16).astype(F32)
        for k in range(KL):
            acc_ref[src_ref[slot * KL + k]] += grads[k * TILE : (k + 1) * TILE]
    dw_ref[0] += dot_tn(own[...], gp)
    dw_ref[1] += dot_tn(mean_ref[...].reshape(ROWS, D), gp)
    db_ref[...] += jnp.sum(gp.astype(F32).reshape(ROWS // 8, 8, D), axis=0)


def rest(src, gp, gm, home, moved, mean, adjacency, w_self):
    return pl.pallas_call(
        rest_kernel,
        out_shape=[
            jax.ShapeDtypeStruct((CL, TILE, D), F32),
            jax.ShapeDtypeStruct((2, D, D), F32),
            jax.ShapeDtypeStruct((8, D), F32),
        ],
        grid_spec=pltpu.PrefetchScalarGridSpec(
            num_scalar_prefetch=1,
            grid=(STEPS,),
            in_specs=[tile_block()] * 3
            + [whole(MIG, TILE, D), tile_block()]
            + [adj_block(0), adj_block(1), adj_block(2), whole(D, D)],
            out_specs=[whole(CL, TILE, D), whole(2, D, D), whole(8, D)],
            scratch_shapes=[pltpu.VMEM((ROWS, D), BF16)],
        ),
        compiler_params=pltpu.CompilerParams(vmem_limit_bytes=40 * 2**20),
    )(src, gp, gm, home, moved, mean, adjacency, adjacency, adjacency, w_self)


def final_kernel(target_ref, acc_in, moved_ref, back_ref, passed_ref, out_ref, acc, tiles, sem):
    blocks = back_ref.shape[0]

    def copies(n, act):
        @pl.when(jnp.logical_and(target_ref[n] >= 0, n < blocks))
        def _():
            act(pltpu.make_async_copy(back_ref.at[n], tiles.at[n], sem.at[n]))

        @pl.when(jnp.logical_and(target_ref[n] >= 0, n >= blocks))
        def _():
            act(pltpu.make_async_copy(passed_ref.at[n - blocks], tiles.at[n], sem.at[n]))

    count = blocks + passed_ref.shape[0]
    loop(0, count, lambda n: copies(n, lambda c: c.start()))
    acc[...] = acc_in[...]
    for j in range(MIG):
        for h in range(2):
            acc[2 * (OWN + j) + h] += moved_ref[j, h * HALF : (h + 1) * HALF].astype(F32)

    def add(n):
        copies(n, lambda c: c.wait())

        @pl.when(target_ref[n] >= 0)
        def _():
            acc[target_ref[n]] += tiles[n].astype(F32)

    loop(0, count, add)
    out_ref[...] = acc[...].astype(BF16)


def finish(target, acc, moved, back, passed):
    count = back.shape[0] + passed.shape[0]
    return pl.pallas_call(
        final_kernel,
        out_shape=jax.ShapeDtypeStruct((2 * CL, HALF, D), BF16),
        grid_spec=pltpu.PrefetchScalarGridSpec(
            num_scalar_prefetch=1,
            grid=(),
            in_specs=[VMEM, VMEM, ANY, ANY],
            out_specs=VMEM,
            scratch_shapes=[
                pltpu.VMEM((2 * CL, HALF, D), F32),
                pltpu.VMEM((count, HALF, D), BF16),
                pltpu.SemaphoreType.DMA((count,)),
            ],
        ),
        compiler_params=pltpu.CompilerParams(vmem_limit_bytes=40 * 2**20),
    )(target, acc.reshape(2 * CL, HALF, D), moved, back, passed)


def requests(owner, local):
    entries = jnp.arange(owner.shape[0], dtype=jnp.int32)
    same = owner[:, None] == owner[None, :]
    second = jnp.any(same & (entries[None, :] < entries[:, None]), axis=1)
    partner = (owner[:, None] ^ 1) == owner[None, :]
    fourth = second & (owner % 2 == 1) & jnp.any(partner & second[None, :], axis=1)
    chip = owner // 2

    column = jnp.where(second, jnp.where(fourth, NDOM + CHIPS + chip, NDOM + chip), owner)
    value = jnp.where(second & ~fourth, (owner % 2) * CL + local, local)
    hit = column[:, None] == jnp.arange(128, dtype=jnp.int32)[None, :]
    row = jnp.sum(jnp.where(hit, value[:, None] + 1, 0), axis=0) - 1
    low = jnp.where(fourth, 3 * NDOM + 2 * owner, jnp.where(second, 6 * chip + 2, 3 * owner))
    high = jnp.where(second & ~fourth, low + 3, low + 1)
    return row, jnp.stack([low, high], axis=1).reshape(-1)


def picks(offset, me):
    core, chip = me % 2, me // 2
    swap = offset % 2
    shift = offset // 2 + ((core ^ swap) & swap)
    place = (chip + shift) % CHIPS
    return jnp.concatenate([place % SIDE, place // SIDE, swap]).astype(jnp.int32)


def body(
    features, w_self, w_neigh, out_bias, cluster_plan, local_source, halo_owner, halo_local,
    adjacency, cotangent,
):
    me = lax.axis_index("dom")
    core, chip = me % 2, me // 2
    home = features[0].reshape(CL, TILE, D)
    cot = cotangent[0].reshape(CL, TILE, D)
    src = local_source.reshape(-1)
    bias = out_bias.reshape(1, D)
    row, blocks = requests(halo_owner.reshape(-1), halo_local.reshape(-1))
    offset = (cluster_plan[OWN:] // CL - me + NDOM) % NDOM
    recv, tables, moved = exchange_forward(picks(offset, me), row.reshape(1, 128), home)
    asked = tables[:, 0, :]
    first = lax.dynamic_slice(asked, (0, me), (NDOM, 1))
    other = lax.dynamic_slice(asked, (0, NDOM + chip), (NDOM, 1))
    fourth = lax.dynamic_slice(asked, (0, NDOM + CHIPS + chip), (NDOM, 1))
    first = jnp.where(first >= 0, 2 * first, -2)
    other = jnp.where((other >= 0) & (other // CL == core), 2 * (other % CL), -2)
    target = jnp.concatenate([first, first + 1, other + core], axis=1).reshape(-1)
    target = jnp.concatenate([target, (other + 1 - core).reshape(-1)])
    target = jnp.where(target >= 0, target, -1)

    def rest_of(extra, recv, moved):
        recv = recv.reshape(NDOM * 3, HALF, D)
        goal = target
        if extra:
            sent = home[jnp.maximum(fourth[:, 0], 0)]
            more = lax.all_to_all(sent, "dom", split_axis=0, concat_axis=0, tiled=True)
            recv = jnp.concatenate([recv, more.reshape(NDOM * 2, HALF, D)])
            wide = jnp.where((fourth >= 0) & (core == 1), 2 * fourth, -2)
            wide = jnp.concatenate([wide, wide + 1], axis=1).reshape(-1)
            wide = jnp.where(wide >= 0, wide, -1)
            goal = jnp.concatenate([target[: NDOM * 3], wide, target[NDOM * 3 :]])
        new, gp, mean, gm, tail, back = middle(
            blocks, src, recv, home, moved, adjacency, cot, w_self, w_neigh, bias
        )
        acc, dw, db = rest(src, gp, gm, home, moved, mean, adjacency, w_self)
        ret, passed, returned, dw_sum, db_sum = exchange_backward(
            picks(NDOM - offset, me), back[: NDOM * 3].reshape(NDOM, WIDE, D), tail, dw, db
        )
        ret = ret.reshape(NDOM * 3, HALF, D)
        if extra:
            sent = back[NDOM * 3 :].reshape(NDOM, TILE, D)
            more = lax.all_to_all(sent, "dom", split_axis=0, concat_axis=0, tiled=True)
            ret = jnp.concatenate([ret, more.reshape(NDOM * 2, HALF, D)])
        grad = finish(goal, acc, returned, ret, passed)
        return new, grad, dw_sum, db_sum

    new, grad, dw_sum, db_sum = lax.cond(
        jnp.any(asked[:, NDOM + CHIPS : NDOM + 2 * CHIPS] >= 0),
        functools.partial(rest_of, True),
        functools.partial(rest_of, False),
        recv,
        moved,
    )
    factor = 1.0 / math.sqrt(NDOM * NREP * CL * TILE)
    return (
        new.reshape(1, CL * TILE, D),
        grad.reshape(1, CL * TILE, D),
        dw_sum[0] * factor,
        dw_sum[1] * factor,
        jnp.sum(db_sum, axis=0) * factor,
    )


def solution(mesh):
    return jax.shard_map(
        body,
        mesh=mesh,
        in_specs=(
            P("rep", "dom", None),
            P(),
            P(),
            P(),
            P("dom"),
            P("dom", None),
            P("dom", None),
            P("dom", None),
            P("dom", None, None, None),
            P("rep", "dom", None),
        ),
        out_specs=(P("rep", "dom", None), P("rep", "dom", None), P(), P(), P()),
        check_vma=False,
    )
```

time: 676 us -> 296 us (0.44)
  Pallas kernels: 0 us -> 278 us
  blocking collectives: 248 us -> 0 us
  waiting for transfers between devices: 135 us -> 0 us
  other arithmetic: 140 us -> 7.29 us
  local copies, waits for them, and re-layouts: 80.2 us -> 8.51 us
  matrix products: 30.2 us -> 0 us
  starting transfers between devices: 25 us -> 0 us
  between operations: 15 us -> 1.4 us
    pallas_call x0 -> x5, Pallas kernels: none -> 278 us  [the longest x1 115 us: exchange_backward(): pl.pallas_call(backward_kernel, out_shape=[jax.ShapeDtypeStruct((NDOM, WI...]
    psum x1 -> x0, blocking collectives: 144 us -> none  [body(): lax.psum((dws_part, dwn_part, bias_part), ('dom', 'rep'))]
    all_gather x2 -> x0, blocking collectives: 90.1 us -> none  [the longest x1 66.7 us: body(): lax.all_gather(halo_local, 'dom', axis=0, tiled=True)]
    scatter-add x3 -> x0, other arithmetic: 88.5 us -> none  [the longest x1 51.1 us: body(): grad_home = grad_home.at[chosen_all].add(incoming)]
    all_to_all x3 -> x0, waiting for transfers between devices: 79.4 us -> none  [the longest x1 79.4 us: body(): lax.all_to_all(filled(halo_chosen, halo_present), 'dom', split_axis=0, co...]
    psum x1 -> x0, waiting for transfers between devices: 55.8 us -> none  [body(): lax.psum((dws_part, dwn_part, bias_part), ('dom', 'rep'))]
    dot_general x8 -> x0, matrix products: 30.2 us -> none  [the longest x1 7.38 us: body(): jnp.einsum('ckij,ckjd->cid', adjacency, neighbour, preferred_element_type...]
    select_n x11 -> x8, other arithmetic: 31.3 us -> 2.24 us  [the longest x1 1.31 us: body(): first = jnp.where(first >= 0, 2 * first, -2)]
  transfers between devices with their start and end apart: 4 -> 0, of which waited for: 2 -> 0; matrix products, arithmetic and copies ran while one was open for 16% -> 0% of each run, Pallas kernels for 0% -> 0%
where the time goes in v1:
time: 296 us; the launch traced here: 295 us
  Pallas kernels  278 us (94%)
  local copies, waits for them, and re-layouts  8.51 us (3%)
  other arithmetic  7.29 us (2%)
    pallas_call x1, Pallas kernels, exchange_backward(): pl.pallas_call(backward_kernel, out_shape=[jax.ShapeDtypeStruct((NDOM, WI...  115 us
    pallas_call x1, Pallas kernels, exchange_forward(): pl.pallas_call(forward_kernel, out_shape=[jax.ShapeDtypeStruct((NDOM, WID...  108 us
    pallas_call x1, Pallas kernels, middle(): pl.pallas_call(middle_kernel, out_shape=[tiles, tiles, tiles, tiles, jax....  22.9 us
    pallas_call x1, Pallas kernels, finish(): pl.pallas_call(final_kernel, out_shape=jax.ShapeDtypeStruct((2 * CL, HALF...  21.3 us
    pallas_call x1, Pallas kernels, rest(): pl.pallas_call(rest_kernel, out_shape=[jax.ShapeDtypeStruct((CL, TILE, D)...  10.3 us

profile of v1, /device:TPU:1, one launch (start us, length us, event | category | flops | bytes accessed | tf_op | source)
XLA Modules:
  0.0 295.3 jit_solution(1441056831026915465)
XLA Ops:
  0.7 0.8 and_select_fusion.23
  1.5 0.8 copy.32
  2.4 0.1 reshape.627
  2.5 0.2 fusion.7
  2.6 0.2 and_reduce_fusion
  2.8 0.8 copy.36
  3.7 0.8 copy.33
  4.6 0.1 select_reduce_fusion
  4.7 108.3 %shard_map.137 = (bf16[32,192,512]{2,1,0:T(8,128)(2,1)}, s32[32,1,128]{2,1,0:T(1,128)S(1)}, bf16[3,128,512]{2,1,0:T(8,128)(2,1)S(1)}) custom-call(s32[9]{0:T(128)S(1)} %pad_add_fusion.6.pick_ref, s32[1,128]{1,0:T(1,128)S(1)} %add_bitcast_fusion.row_ref, bf16[16,128,512]{2,1,0:T(8,128)(2,1)} %bitcast.80), custom_call_target="tpu_custom_call" | custom-call | tf_op jit(solution)/shard_map/pallas_call | solution.py:246
  112.9 0.7 fusion.8
  114.3 1.3 fusion.5
  115.7 0.1 copy.37
  115.8 0.1 reshape.631
  116.0 0.1 copy.35
  116.1 0.1 reshape.628
  116.2 175.4 %conditional.1 = (bf16[16,128,512]{2,1,0:T(8,128)(2,1)}, f32[2,512,512]{2,1,0:T(8,128)}, f32[8,512]{1,0:T(8,128)S(1)}, bf16[1,2048,512]{2,1,0:T(8,128)(2,1)}) conditional(s32[]{:T(128)} %convert_element_type.3, (bf16[32,192,512]{2,1,0:T(8,128)(2,1)}, s32[64]{0:T(128)S(1)}, s32[48]{0:T(128)S(1)}, bf16[16,128,512]{2,1,0:T(8,128)(2,1)}, ...), branch_computations={%region_4.5_spmd, %region_5.6_spmd} | conditional | flops 10487777 | bytes 234931712 | solution.py:714
  116.5 22.9 %branch_0_fun.4 = (bf16[16,128,512]{2,1,0:T(8,128)(2,1)}, bf16[16,128,512]{2,1,0:T(8,128)(2,1)S(1)}, bf16[16,128,512]{2,1,0:T(8,128)(2,1)S(1)}, bf16[16,128,512]...) custom-call(s32[64]{0:T(128)S(1)} %get-tuple-element.71.block_ref, ...), custom_call_target="tpu_custom_call" | custom-call | tf_op jit(solution)/shard_map/cond/branch_0_fun/pallas_call | solution.py:502
  139.5 10.3 %branch_0_fun.5 = (f32[16,128,512]{2,1,0:T(8,128)S(1)}, f32[2,512,512]{2,1,0:T(8,128)S(1)}, f32[8,512]{1,0:T(8,128)S(1)}) custom-call(s32[48]{0:T(128)S(1)} %get-tuple-element.72.src_ref, bf16[16,128,512]{2,1,0:T(8,128)(2,1)S(1)} %get-tuple-element.86.gp_ref, bf16[16,128,512]{2,1,0:T(8,128)(2,1)S(1)} %get-tuple-element.87.gm_ref, ...), custom_call_target="tpu_custom_call" | custom-call | tf_op jit(solution)/shard_map/cond/branch_0_fun/pallas_call | solution.py:570
  149.8 115.0 %branch_0_fun.6 = (bf16[32,192,512]{2,1,0:T(8,128)(2,1)S(1)}, bf16[32,64,512]{2,1,0:T(8,128)(2,1)S(1)}, bf16[3,128,512]{2,1,0:T(8,128)(2,1)S(1)}, f32[2,512,512]{2,1,0:T(8,128)}, f32[8,512]{1,0:T(8,128)S(1)}) custom-call(s32[9]{0:T(128)S(1)} %pad_add_fusion.pick_ref, bf16[32,192,512]{2,1,0:T(8,128)(2,1)S(1)} %bitcast.56, ...), custom_call_target="tpu_custom_call" | custom-call | tf_op jit(solution)/shard_map/cond/branch_0_fun/pallas_call | solution.py:392
  264.8 2.7 copy-done
  267.5 2.8 copy-done.1
  270.3 21.3 %branch_0_fun.7 = bf16[32,64,512]{2,1,0:T(8,128)(2,1)} custom-call(s32[128]{0:T(128)S(1)} %get-tuple-element.93.target_ref, f32[32,64,512]{2,1,0:T(8,128)S(1)} %bitcast.60, bf16[3,128,512]{2,1,0:T(8,128)(2,1)S(1)} %get-tuple-element.95.moved_ref, bf16[96,64,512]{2,1,0:T(8,128)(2,1)S(1)} %bitcast.57, bf16[32,64,512]{2,1,0:T(8,128)(2,1)S(1)} %get-tuple-element.97.passed_ref), custom_call_target="tpu_custom_call" | custom-call | tf_op jit(solution)/shard_map/cond/branch_0_fun/pallas_call | solution.py:622
  291.7 0.6 broadcast_multiply_fusion
  292.2 3.1 %multiply_bitcast_fusion = (f32[512,512]{1,0:T(8,128)}, f32[512,512]{1,0:T(8,128)}) fusion(f32[2,512,512]{2,1,0:T(8,128)} %get-tuple-element.145), kind=kLoop, calls=%fused_computation.46 | loop fusion | flops 524288 | bytes 4194304 | tf_op jit(solution)/shard_map/mul | solution.py:726
  (26 shorter events, 0.7 us)
Async XLA Ops:
  116.5 22.9 %copy-start.9 = (bf16[16,5,128,128]{3,2,1,0:T(8,128)(2,1)S(1)}, bf16[16,5,128,128]{3,2,1,0:T(8,128)(2,1)}, u32[]{:S(2)}) copy-start(bf16[16,5,128,128]{3,2,1,0:T(8,128)(2,1)} %get-tuple-element.76.refs_18_.a0_ref.a1_ref.a2_ref) | copy-start | bytes 7864324 | tf_op jit(solution)/shard_map/cond
  116.5 22.9 %copy-start.11 = (bf16[16,128,512]{2,1,0:T(8,128)(2,1)S(1)}, bf16[16,128,512]{2,1,0:T(8,128)(2,1)}, u32[]{:S(2)}) copy-start(bf16[16,128,512]{2,1,0:T(8,128)(2,1)} %get-tuple-element.74.refs_16_.home_ref) | copy-start | bytes 6291460 | tf_op jit(solution)/shard_map/cond
  116.5 22.9 %copy-start.14 = (bf16[512,512]{1,0:T(8,128)(2,1)S(1)}, bf16[512,512]{1,0:T(8,128)(2,1)}, u32[]{:S(2)}) copy-start(bf16[512,512]{1,0:T(8,128)(2,1)} %get-tuple-element.78.refs_20_.w_ref) | copy-start | bytes 1572868 | tf_op jit(solution)/shard_map/cond
  264.8 2.7 copy-start
  267.5 2.8 copy-start.1

commit v2 on v1

--- a/solution.py
+++ b/solution.py
@@ -24,6 +24,7 @@
 GROUP = 4
 STEPS = CL // GROUP
 ROWS = GROUP * TILE
+FACTOR = 1.0 / math.sqrt(NDOM * NREP * CL * TILE)
 MESH = pl.DeviceIdType.MESH
 F32 = jnp.float32
 BF16 = jnp.bfloat16
@@ -265,11 +266,15 @@
     )(pick, row, home)
 
 
+NEAR = CL * KL
+
+
 def backward_kernel(
-    pick_ref, back_ref, tail_ref, dw_ref, db_ref,
-    ret_ref, passed_ref, moved_ref, out_ref, bias_ref,
+    pick_ref, order_ref, back_ref, tail_ref, gp_ref, gm_ref, mean_ref, home_ref, moved_in, adj_ref, w_ref,
+    ret_ref, passed_ref, moved_ref, acc_ref, out_ref, bias_ref,
     along_x, picked, along_y, lanes, shift_sems,
     r1, b1, s1, r2, b2, s2, r3, b3, sums, half_sems, tile_sems, pass_sems, local_sems,
+    gp, gm, mean, own, adj, w, dw, db, acc, running,
 ):
     here = Place()
     me, core, chip, rep, partner = here.me, here.core, here.chip, here.rep, here.partner
@@ -288,6 +293,22 @@
     loop(1, NREP, greet_z)
     keep = pltpu.make_async_copy(back_ref.at[me], ret_ref.at[me], local_sems.at[0])
     keep.start()
+    loads = [
+        pltpu.make_async_copy(src, dst, local_sems.at[1 + n])
+        for n, (src, dst) in enumerate(
+            [
+                (gp_ref, gp),
+                (home_ref.at[pl.ds(0, OWN)], own.at[pl.ds(0, OWN)]),
+                (moved_in, own.at[pl.ds(OWN, MIG)]),
+                (mean_ref, mean),
+                (gm_ref, gm),
+                (w_ref, w),
+                (adj_ref, adj),
+            ]
+        )
+    ]
+    for copy in loads:
+        copy.start()
     along_x[here.x] = tail_ref[...]
     pl.semaphore_wait(barrier, NDOM - 1 + NREP - 1)
 
@@ -297,17 +318,32 @@
     shift = Shift(here, pick_ref, along_x, picked, along_y, lanes, shift_sems)
     halves = Exchange(here, back_ref, ret_ref, half_sems.at[0], half_sems.at[1], TILE, WIDE)
     tiles = Exchange(here, back_ref, ret_ref, tile_sems.at[0], tile_sems.at[1], 0, TILE)
-
-    c_dw = send(dw_ref.at[1 - core], r1, 0, partner, rep)
-    c_db = send(db_ref, b1, 1, partner, rep)
+    shift.start_x()
+    halves.start(0, HALF // CHUNK)
+
+    dw[...] = jnp.zeros_like(dw)
+    db[...] = jnp.zeros_like(db)
+    for copy in loads[:4]:
+        copy.wait()
+
+    def weights(g):
+        rows = pl.ds(g * GROUP, GROUP)
+        grad = gp[rows].reshape(ROWS, D)
+        dw[0] += dot_tn(own[rows].reshape(ROWS, D), grad)
+        dw[1] += dot_tn(mean[rows].reshape(ROWS, D), grad)
+        db[...] += jnp.sum(grad.astype(F32).reshape(ROWS // 8, 8, D), axis=0)
+
+    loop(0, STEPS, weights)
+
+    c_dw = send(dw.at[1 - core], r1, 0, partner, rep)
+    c_db = send(db, b1, 1, partner, rep)
     c_dw.start()
     c_db.start()
-    shift.start_x()
-    halves.start(0, HALF // CHUNK)
+    tiles.start(0, 1)
     c_db.wait()
     c_dw.wait()
-    s1[...] = dw_ref[core] + r1[...]
-    b2[rep] = db_ref[...] + b1[...]
+    s1[...] = dw[core] + r1[...]
+    b2[rep] = db[...] + b1[...]
 
     def z_dw(t):
         z = z_peer(t)
@@ -319,8 +355,20 @@
     loop(1, NREP, lambda t: z_dw(t).start())
     loop(1, NREP, lambda t: z_db(t).start())
     r2[rep] = s1[pl.ds(pl.multiple_of(rep * ZROWS, ZROWS), ZROWS)]
-    tiles.start(0, 2)
+    tiles.start(1, 2)
     shift.start_y()
+
+    for copy in loads[4:]:
+        copy.wait()
+
+    def kept(g):
+        rows = pl.ds(g * GROUP, GROUP)
+        part = dot_nt(gp[rows].reshape(ROWS, D), w[...]) + gm[rows].reshape(ROWS, D).astype(F32)
+        acc[rows] = part.reshape(GROUP, TILE, D)
+
+    loop(0, STEPS, kept)
+    acc[pl.ds(OWN, MIG)] = jnp.zeros((MIG, TILE, D), F32)
+
     loop(1, NREP, lambda t: z_db(t).wait())
     loop(1, NREP, lambda t: z_dw(t).wait())
     s2[...] = (r2[0] + r2[1]) + (r2[2] + r2[3])
@@ -338,6 +386,22 @@
     r3[chip] = s2[pl.ds(pl.multiple_of(chip * CROWS, CROWS), CROWS)]
     tiles.start(2, 4)
     shift.start_lane()
+
+    running[0] = jnp.zeros((TILE, D), F32)
+
+    def near(n):
+        e = order_ref[n]
+        running[n + 1] = running[n] + dot_tn(adj[e // KL, e % KL], gm[e // KL])
+
+    loop(0, NEAR, near)
+
+    def settle(h):
+        acc[h] += running[order_ref[NEAR + h + 1]] - running[order_ref[NEAR + h]]
+
+    loop(0, CL, settle)
+    store = pltpu.make_async_copy(acc, acc_ref, local_sems.at[8])
+    store.start()
+
     loop(1, CHIPS, lambda t: p_dw(t).wait())
     total = r3[0]
     for q in range(1, CHIPS):
@@ -386,20 +450,23 @@
     for n in range(NPEER):
         tiles.every(n).wait()
     last.wait()
-
-
-def exchange_backward(pick, back, tail, dw, db):
+    store.wait()
+
+
+def exchange_backward(pick, order, back, tail, gp, gm, mean, home, moved, adjacency, w_self):
+    tiles = pltpu.VMEM((CL, TILE, D), BF16)
     return pl.pallas_call(
         backward_kernel,
         out_shape=[
             jax.ShapeDtypeStruct((NDOM, WIDE, D), BF16),
             jax.ShapeDtypeStruct((NDOM, HALF, D), BF16),
             jax.ShapeDtypeStruct((MIG, TILE, D), BF16),
+            jax.ShapeDtypeStruct((CL, TILE, D), F32),
             jax.ShapeDtypeStruct((2, D, D), F32),
             jax.ShapeDtypeStruct((8, D), F32),
         ],
-        in_specs=[SMEM, ANY, VMEM, VMEM, VMEM],
-        out_specs=[ANY, ANY, VMEM, VMEM, VMEM],
+        in_specs=[SMEM, SMEM, ANY, VMEM] + [ANY] * 7,
+        out_specs=[ANY, ANY, VMEM, ANY, VMEM, VMEM],
         scratch_shapes=SHIFT_SCRATCH
         + [
             pltpu.VMEM((D, D), F32),
@@ -414,12 +481,22 @@
             EXCHANGE_SEMS,
             EXCHANGE_SEMS,
             pltpu.SemaphoreType.DMA((2, NDOM)),
-            pltpu.SemaphoreType.DMA((1,)),
+            pltpu.SemaphoreType.DMA((9,)),
+            tiles,
+            tiles,
+            tiles,
+            tiles,
+            pltpu.VMEM((CL, KL + KH, TILE, TILE), BF16),
+            pltpu.VMEM((D, D), BF16),
+            pltpu.VMEM((2, D, D), F32),
+            pltpu.VMEM((8, D), F32),
+            pltpu.VMEM((CL, TILE, D), F32),
+            pltpu.VMEM((NEAR + 1, TILE, D), F32),
         ],
         compiler_params=pltpu.CompilerParams(
-            collective_id=1, has_side_effects=True, vmem_limit_bytes=32 * 2**20
+            collective_id=1, has_side_effects=True, vmem_limit_bytes=52 * 2**20
         ),
-    )(pick, back, tail, dw, db)
+    )(pick, order, back, tail, gp, gm, mean, home, moved, adjacency, w_self)
 
 
 def tile_block(width=D):
@@ -533,108 +610,79 @@
     )
 
 
-def rest_kernel(
-    src_ref, gp_ref, gm_ref, home_ref, moved_ref, mean_ref, a0_ref, a1_ref, a2_ref, w_ref,
-    acc_ref, dw_ref, db_ref, own,
-):
+FOUR = 4
+
+
+def final_kernel(first_ref, other_ref, more_ref, acc_ref, moved_ref, back_ref, passed_ref, *refs):
+    extra_ref = refs[0] if len(refs) == 8 else None
+    dw_ref, db_ref, out_ref, dws_ref, dwn_ref, bias_ref, acc = refs[-7:]
     g = pl.program_id(0)
+    here_half = lax.rem(lax.axis_index("dom"), 2)
+    dws_ref[...] = dw_ref[0] * FACTOR
+    dwn_ref[...] = dw_ref[1] * FACTOR
 
     @pl.when(g == 0)
     def _():
-        acc_ref[...] = jnp.zeros_like(acc_ref)
-        dw_ref[...] = jnp.zeros_like(dw_ref)
-        db_ref[...] = jnp.zeros_like(db_ref)
-
-    gp = gp_ref[...].reshape(ROWS, D)
-    gm = gm_ref[...].reshape(ROWS, D)
-    own_grad = (dot_nt(gp, w_ref[...]) + gm.astype(F32)).astype(BF16)
-    for i in range(GROUP):
-        part = own_grad[i * TILE : (i + 1) * TILE]
-        slot = g * GROUP + i
-        own[pl.ds(i * TILE, TILE)] = own_tile(i, g, home_ref[i], moved_ref)
-
-        @pl.when(slot < OWN)
+        bias_ref[...] = jnp.sum(db_ref[...], axis=0, keepdims=True) * FACTOR
+        acc[...] = acc_ref[...]
+        for j in range(MIG):
+            acc[OWN + j] += moved_ref[j].astype(F32)
+
+    for n in range(FOUR):
+        c = g * FOUR + n
+        first, other = first_ref[c], other_ref[c]
+
+        @pl.when(first >= 0)
         def _():
-            acc_ref[slot] += part.astype(F32)
-
-        adj = jnp.concatenate([a0_ref[i, 0], a1_ref[i, 0], a2_ref[i, 0]], axis=1)
-        grads = dot_tn(adj, gm[i * TILE : (i + 1) * TILE]).astype(BF16).astype(F32)
-        for k in range(KL):
-            acc_ref[src_ref[slot * KL + k]] += grads[k * TILE : (k + 1) * TILE]
-    dw_ref[0] += dot_tn(own[...], gp)
-    dw_ref[1] += dot_tn(mean_ref[...].reshape(ROWS, D), gp)
-    db_ref[...] += jnp.sum(gp.astype(F32).reshape(ROWS // 8, 8, D), axis=0)
-
-
-def rest(src, gp, gm, home, moved, mean, adjacency, w_self):
+            acc[first] += back_ref[n, pl.ds(0, TILE)].astype(F32)
+
+        @pl.when(other >= 0)
+        def _():
+            rows = pl.ds(pl.multiple_of(here_half * HALF, HALF), HALF)
+            acc[other, rows] += back_ref[n, pl.ds(TILE, HALF)].astype(F32)
+            rows = pl.ds(pl.multiple_of((1 - here_half) * HALF, HALF), HALF)
+            acc[other, rows] += passed_ref[n].astype(F32)
+
+        if extra_ref is not None:
+            more = more_ref[c]
+
+            @pl.when(more >= 0)
+            def _():
+                acc[more] += extra_ref[n].astype(F32)
+
+    @pl.when(g == NDOM // FOUR - 1)
+    def _():
+        out_ref[...] = acc[...].astype(BF16)
+
+
+def finish(first, other, more, acc, moved, back, passed, extra, dw, db):
+    steps = NDOM // FOUR
+
+    def four(rows):
+        return pl.BlockSpec((FOUR, rows, D), lambda g, *_: (g, 0, 0))
+
+    extras = [] if extra is None else [extra]
     return pl.pallas_call(
-        rest_kernel,
+        final_kernel,
         out_shape=[
-            jax.ShapeDtypeStruct((CL, TILE, D), F32),
-            jax.ShapeDtypeStruct((2, D, D), F32),
-            jax.ShapeDtypeStruct((8, D), F32),
+            jax.ShapeDtypeStruct((CL, TILE, D), BF16),
+            jax.ShapeDtypeStruct((D, D), F32),
+            jax.ShapeDtypeStruct((D, D), F32),
+            jax.ShapeDtypeStruct((1, D), F32),
         ],
         grid_spec=pltpu.PrefetchScalarGridSpec(
-            num_scalar_prefetch=1,
-            grid=(STEPS,),
-            in_specs=[tile_block()] * 3
-            + [whole(MIG, TILE, D), tile_block()]
-            + [adj_block(0), adj_block(1), adj_block(2), whole(D, D)],
-            out_specs=[whole(CL, TILE, D), whole(2, D, D), whole(8, D)],
-            scratch_shapes=[pltpu.VMEM((ROWS, D), BF16)],
+            num_scalar_prefetch=3,
+            grid=(steps,),
+            in_specs=[whole(CL, TILE, D), whole(MIG, TILE, D), four(WIDE), four(HALF)]
+            + [four(TILE)] * len(extras)
+            + [pl.BlockSpec((2, D // steps, D), lambda g, *_: (0, g, 0)), whole(8, D)],
+            out_specs=[whole(CL, TILE, D)]
+            + [pl.BlockSpec((D // steps, D), lambda g, *_: (g, 0))] * 2
+            + [whole(1, D)],
+            scratch_shapes=[pltpu.VMEM((CL, TILE, D), F32)],
         ),
         compiler_params=pltpu.CompilerParams(vmem_limit_bytes=40 * 2**20),
-    )(src, gp, gm, home, moved, mean, adjacency, adjacency, adjacency, w_self)
-
-
-def final_kernel(target_ref, acc_in, moved_ref, back_ref, passed_ref, out_ref, acc, tiles, sem):
-    blocks = back_ref.shape[0]
-
-    def copies(n, act):
-        @pl.when(jnp.logical_and(target_ref[n] >= 0, n < blocks))
-        def _():
-            act(pltpu.make_async_copy(back_ref.at[n], tiles.at[n], sem.at[n]))
-
-        @pl.when(jnp.logical_and(target_ref[n] >= 0, n >= blocks))
-        def _():
-            act(pltpu.make_async_copy(passed_ref.at[n - blocks], tiles.at[n], sem.at[n]))
-
-    count = blocks + passed_ref.shape[0]
-    loop(0, count, lambda n: copies(n, lambda c: c.start()))
-    acc[...] = acc_in[...]
-    for j in range(MIG):
-        for h in range(2):
-            acc[2 * (OWN + j) + h] += moved_ref[j, h * HALF : (h + 1) * HALF].astype(F32)
-
-    def add(n):
-        copies(n, lambda c: c.wait())
-
-        @pl.when(target_ref[n] >= 0)
-        def _():
-            acc[target_ref[n]] += tiles[n].astype(F32)
-
-    loop(0, count, add)
-    out_ref[...] = acc[...].astype(BF16)
-
-
-def finish(target, acc, moved, back, passed):
-    count = back.shape[0] + passed.shape[0]
-    return pl.pallas_call(
-        final_kernel,
-        out_shape=jax.ShapeDtypeStruct((2 * CL, HALF, D), BF16),
-        grid_spec=pltpu.PrefetchScalarGridSpec(
-            num_scalar_prefetch=1,
-            grid=(),
-            in_specs=[VMEM, VMEM, ANY, ANY],
-            out_specs=VMEM,
-            scratch_shapes=[
-                pltpu.VMEM((2 * CL, HALF, D), F32),
-                pltpu.VMEM((count, HALF, D), BF16),
-                pltpu.SemaphoreType.DMA((count,)),
-            ],
-        ),
-        compiler_params=pltpu.CompilerParams(vmem_limit_bytes=40 * 2**20),
-    )(target, acc.reshape(2 * CL, HALF, D), moved, back, passed)
+    )(first, other, more, acc, moved, back, passed, *extras, dw, db)
 
 
 def requests(owner, local):
@@ -652,6 +700,19 @@
     low = jnp.where(fourth, 3 * NDOM + 2 * owner, jnp.where(second, 6 * chip + 2, 3 * owner))
     high = jnp.where(second & ~fourth, low + 3, low + 1)
     return row, jnp.stack([low, high], axis=1).reshape(-1)
+
+
+def sorted_near(src):
+    entries = jnp.arange(NEAR, dtype=jnp.int32)
+    ahead = (src[None, :] < src[:, None]) | (
+        (src[None, :] == src[:, None]) & (entries[None, :] < entries[:, None])
+    )
+    rank = jnp.sum(ahead.astype(jnp.int32), axis=1)
+    order = jnp.sum(jnp.where(rank[None, :] == entries[:, None], entries[None, :], 0), axis=1)
+    begins = jnp.sum(
+        (src[None, :] < jnp.arange(CL + 1, dtype=jnp.int32)[:, None]).astype(jnp.int32), axis=1
+    )
+    return jnp.concatenate([order, begins])
 
 
 def picks(offset, me):
@@ -676,55 +737,41 @@
     offset = (cluster_plan[OWN:] // CL - me + NDOM) % NDOM
     recv, tables, moved = exchange_forward(picks(offset, me), row.reshape(1, 128), home)
     asked = tables[:, 0, :]
-    first = lax.dynamic_slice(asked, (0, me), (NDOM, 1))
-    other = lax.dynamic_slice(asked, (0, NDOM + chip), (NDOM, 1))
-    fourth = lax.dynamic_slice(asked, (0, NDOM + CHIPS + chip), (NDOM, 1))
-    first = jnp.where(first >= 0, 2 * first, -2)
-    other = jnp.where((other >= 0) & (other // CL == core), 2 * (other % CL), -2)
-    target = jnp.concatenate([first, first + 1, other + core], axis=1).reshape(-1)
-    target = jnp.concatenate([target, (other + 1 - core).reshape(-1)])
-    target = jnp.where(target >= 0, target, -1)
+    first = lax.dynamic_slice(asked, (0, me), (NDOM, 1)).reshape(-1)
+    other = lax.dynamic_slice(asked, (0, NDOM + chip), (NDOM, 1)).reshape(-1)
+    more = lax.dynamic_slice(asked, (0, NDOM + CHIPS + chip), (NDOM, 1)).reshape(-1)
+    other = jnp.where((other >= 0) & (other // CL == core), other % CL, -1)
+    more_here = jnp.where(core == 1, more, -1)
+    order = sorted_near(src)
 
     def rest_of(extra, recv, moved):
         recv = recv.reshape(NDOM * 3, HALF, D)
-        goal = target
         if extra:
-            sent = home[jnp.maximum(fourth[:, 0], 0)]
-            more = lax.all_to_all(sent, "dom", split_axis=0, concat_axis=0, tiled=True)
-            recv = jnp.concatenate([recv, more.reshape(NDOM * 2, HALF, D)])
-            wide = jnp.where((fourth >= 0) & (core == 1), 2 * fourth, -2)
-            wide = jnp.concatenate([wide, wide + 1], axis=1).reshape(-1)
-            wide = jnp.where(wide >= 0, wide, -1)
-            goal = jnp.concatenate([target[: NDOM * 3], wide, target[NDOM * 3 :]])
+            sent = home[jnp.maximum(more, 0)]
+            got = lax.all_to_all(sent, "dom", split_axis=0, concat_axis=0, tiled=True)
+            recv = jnp.concatenate([recv, got.reshape(NDOM * 2, HALF, D)])
         new, gp, mean, gm, tail, back = middle(
             blocks, src, recv, home, moved, adjacency, cot, w_self, w_neigh, bias
         )
-        acc, dw, db = rest(src, gp, gm, home, moved, mean, adjacency, w_self)
-        ret, passed, returned, dw_sum, db_sum = exchange_backward(
-            picks(NDOM - offset, me), back[: NDOM * 3].reshape(NDOM, WIDE, D), tail, dw, db
+        ret, passed, returned, acc, dw, db = exchange_backward(
+            picks(NDOM - offset, me), order, back[: NDOM * 3].reshape(NDOM, WIDE, D), tail,
+            gp, gm, mean, home, moved, adjacency, w_self,
         )
-        ret = ret.reshape(NDOM * 3, HALF, D)
+        got = None
         if extra:
             sent = back[NDOM * 3 :].reshape(NDOM, TILE, D)
-            more = lax.all_to_all(sent, "dom", split_axis=0, concat_axis=0, tiled=True)
-            ret = jnp.concatenate([ret, more.reshape(NDOM * 2, HALF, D)])
-        grad = finish(goal, acc, returned, ret, passed)
-        return new, grad, dw_sum, db_sum
-
-    new, grad, dw_sum, db_sum = lax.cond(
+            got = lax.all_to_all(sent, "dom", split_axis=0, concat_axis=0, tiled=True)
+        return new, *finish(first, other, more_here, acc, returned, ret, passed, got, dw, db)
+
+    new, grad, dws, dwn, db = lax.cond(
         jnp.any(asked[:, NDOM + CHIPS : NDOM + 2 * CHIPS] >= 0),
         functools.partial(rest_of, True),
         functools.partial(rest_of, False),
         recv,
         moved,
     )
-    factor = 1.0 / math.sqrt(NDOM * NREP * CL * TILE)
     return (
-        new.reshape(1, CL * TILE, D),
-        grad.reshape(1, CL * TILE, D),
-        dw_sum[0] * factor,
-        dw_sum[1] * factor,
-        jnp.sum(db_sum, axis=0) * factor,
+        new.reshape(1, CL * TILE, D), grad.reshape(1, CL * TILE, D), dws, dwn, db.reshape(D)
     )
 
 

time: 296 us -> 287 us (0.970)
  Pallas kernels: 278 us -> 266 us
  local copies, waits for them, and re-layouts: 8.51 us -> 16.7 us
  other arithmetic: 7.29 us -> 2.69 us
    pallas_call x2 -> x1, Pallas kernels: 31.6 us -> 8.7 us  [finish(): pl.pallas_call(final_kernel, out_shape=[jax.ShapeDtypeStruct((CL, TILE, D...]
    pallas_call x1, Pallas kernels: 115 us -> 126 us  [exchange_backward(): pl.pallas_call(backward_kernel, out_shape=[jax.ShapeDtypeStruct((NDOM, WI...]
    cond x10 -> x20, local copies, waits for them, and re-layouts: 5.5 us -> 12 us
    mul x2 -> x0, other arithmetic: 3.67 us -> none  [the longest x1 3.09 us: body(): dw_sum[1] * factor]
where the time goes in v2:
time: 287 us
  Pallas kernels  266 us (93%)
  local copies, waits for them, and re-layouts  16.7 us (6%)
    pallas_call x1, Pallas kernels, exchange_backward(): pl.pallas_call(backward_kernel, out_shape=[jax.ShapeDtypeStruct((NDOM, WI...  126 us
    pallas_call x1, Pallas kernels, exchange_forward(): pl.pallas_call(forward_kernel, out_shape=[jax.ShapeDtypeStruct((NDOM, WID...  108 us
    pallas_call x1, Pallas kernels, middle(): pl.pallas_call(middle_kernel, out_shape=[tiles, tiles, tiles, tiles, jax....  22.8 us
    cond x20, local copies, waits for them, and re-layouts  12 us
    pallas_call x1, Pallas kernels, finish(): pl.pallas_call(final_kernel, out_shape=[jax.ShapeDtypeStruct((CL, TILE, D...  8.7 us

profile of v2, /device:TPU:1, one launch (start us, length us, event | category | flops | bytes accessed | tf_op | source)
XLA Modules:
  0.0 287.0 jit_solution(13745115953393890232)
XLA Ops:
  0.7 0.8 and_select_fusion.19
  1.5 0.8 copy.25
  2.5 0.2 fusion.7
  2.7 0.2 and_reduce_fusion
  2.9 0.8 copy.29
  3.7 0.1 convert_reduce_fusion.1
  3.8 0.2 convert_reduce_fusion
  4.0 0.1 select_reduce_fusion
  4.2 0.8 copy.26
  5.3 0.1 reshape.331
  5.4 108.3 %shard_map.137 = (bf16[32,192,512]{2,1,0:T(8,128)(2,1)}, s32[32,1,128]{2,1,0:T(1,128)S(1)}, bf16[3,128,512]{2,1,0:T(8,128)(2,1)S(1)}) custom-call(s32[9]{0:T(128)S(1)} %pad_add_fusion.3.pick_ref, s32[1,128]{1,0:T(1,128)S(1)} %add_bitcast_fusion.row_ref, bf16[16,128,512]{2,1,0:T(8,128)(2,1)} %bitcast.49), custom_call_target="tpu_custom_call" | custom-call | tf_op jit(solution)/shard_map/pallas_call | solution.py:247
  113.7 0.7 fusion.8
  115.0 1.9 dynamic-slice_reduce_fusion
  117.0 169.9 %conditional.1 = (bf16[16,128,512]{2,1,0:T(8,128)(2,1)}, bf16[16,128,512]{2,1,0:T(8,128)(2,1)}, f32[512,512]{1,0:T(8,128)}, f32[512,512]{1,0:T(8,128)}, f32[1,512]{1,0:T(1,128)}) conditional(s32[]{:T(128)} %convert_element_type.9, (bf16[32,192,512]{2,1,0:T(8,128)(2,1)}, s32[64]{0:T(128)S(1)}, s32[48]{0:T(128)S(1)}, bf16[16,128,512]{2,1,0:T(8,128)(2,1)}, ...), branch_computations={%region_7.8_spmd, %region_8.9_spmd} | conditional | flops 5244156 | bytes 199249120 | solution.py:766
  117.3 22.8 %branch_0_fun.3 = (bf16[16,128,512]{2,1,0:T(8,128)(2,1)}, bf16[16,128,512]{2,1,0:T(8,128)(2,1)S(1)}, bf16[16,128,512]{2,1,0:T(8,128)(2,1)S(1)}, bf16[16,128,512]...) custom-call(s32[64]{0:T(128)S(1)} %get-tuple-element.66.block_ref, ...), custom_call_target="tpu_custom_call" | custom-call | tf_op jit(solution)/shard_map/cond/branch_0_fun/pallas_call | solution.py:579
  140.1 2.6 copy-done
  142.8 1.3 copy-done.8
  144.1 1.3 copy-done.9
  145.4 1.3 copy-done.10
  146.8 126.1 %branch_0_fun.4 = (bf16[32,192,512]{2,1,0:T(8,128)(2,1)}, bf16[32,64,512]{2,1,0:T(8,128)(2,1)}, bf16[3,128,512]{2,1,0:T(8,128)(2,1)S(1)}, f32[16,128,512]{2,1,0:...) custom-call(s32[9]{0:T(128)S(1)} %pad_add_fusion.pick_ref, s32[65]{0:T(128)S(1)} %get-tuple-element.82.order_ref, ...), custom_call_target="tpu_custom_call" | custom-call | tf_op jit(solution)/shard_map/cond/branch_0_fun/pallas_call | solution.py:458
  272.8 2.2 copy-done.2
  275.0 1.6 copy-done.11
  276.6 1.6 copy-done.12
  278.2 8.7 %branch_0_fun.5 = (bf16[16,128,512]{2,1,0:T(8,128)(2,1)}, f32[512,512]{1,0:T(8,128)}, f32[512,512]{1,0:T(8,128)}, f32[1,512]{1,0:T(1,128)}) custom-call(s32[32]{0:T(128)S(1)} %get-tuple-element.77.first_ref, s32[32]{0:T(128)S(1)} %get-tuple-element.78.other_ref, s32[32]{0:T(128)S(1)} %get-tuple-element.79.more_ref, f32[16,128,512]{2,1,0:T(8,128)S(1)} %copy-done.2, ...), custom_call_target="tpu_custom_call" | custom-call | tf_op jit(solution)/shard_map/cond/branch_0_fun/pallas_call | solution.py:665
  (31 shorter events, 0.9 us)
Async XLA Ops:
  117.3 29.4 %copy-start.13 = (bf16[16,128,512]{2,1,0:T(8,128)(2,1)S(1)}, bf16[16,128,512]{2,1,0:T(8,128)(2,1)}, u32[]{:S(2)}) copy-start(bf16[16,128,512]{2,1,0:T(8,128)(2,1)} %get-tuple-element.69.refs_16_.home_ref) | copy-start | bytes 6291460 | tf_op jit(solution)/shard_map/cond
  117.3 29.4 %copy-start.16 = (bf16[16,5,128,128]{3,2,1,0:T(8,128)(2,1)S(1)}, bf16[16,5,128,128]{3,2,1,0:T(8,128)(2,1)}, u32[]{:S(2)}) copy-start(bf16[16,5,128,128]{3,2,1,0:T(8,128)(2,1)} %get-tuple-element.71.refs_18_.adj_ref) | copy-start | bytes 7864324 | tf_op jit(solution)/shard_map/cond
  117.3 29.4 %copy-start.20 = (bf16[512,512]{1,0:T(8,128)(2,1)S(1)}, bf16[512,512]{1,0:T(8,128)(2,1)}, u32[]{:S(2)}) copy-start(bf16[512,512]{1,0:T(8,128)(2,1)} %get-tuple-element.73.refs_20_.w_ref) | copy-start | bytes 1572868 | tf_op jit(solution)/shard_map/cond
  140.1 2.7 copy-start
  142.8 1.3 copy-start.8
  144.1 1.3 copy-start.9
  145.4 1.3 copy-start.10
  272.8 2.2 copy-start.2
  275.0 1.6 copy-start.11
  276.6 1.6 copy-start.12
